TPU v7x, 32 devices: a whole 2x2x4 slice. The times are simulated.
32 devices in a mesh: seq: 8 (over z, y), blk: 2 (over x), clip: 2 (over core).
Axes of the slice: x: 2, y: 2, z: 4, core: 2. Of those that a mesh axis runs over, the one named last changes fastest.
Arguments:
- modulated: bfloat16 [24576, 3072], P(('clip', 'seq', 'blk')), parts along dimension 0, may hold values from -16 to 16
- mod_gate: float32 [6144], P('clip'), parts along dimension 0, may hold values from 0.5 to 1.5
- w_qkv: bfloat16 [3072, 4608], P(None, 'blk'), may hold values from -0.109375 to 0.109375
- w_out: bfloat16 [1536, 3072], P(None, 'blk'), may hold values from -0.15625 to 0.15625
- kv_tiles: int32 [64, 6], P('clip'), parts along dimension 0, may hold values from 0 to 31, as said below
- kv_count: int32 [64], P('clip'), parts along dimension 0, may hold values from 1 to 6, as said below
Outputs:
- update: bfloat16 [24576, 3072], P(('clip', 'seq', 'blk')), parts along dimension 0
There are 2 independent parts, one for each index of `clip`. A program takes and returns all parts, laid end to end along the dimension named above; an argument that names none is the same for every part. Nothing has to cross between parts.
Inputs may be any that keep to these rules, and one draw needn't show every extreme that they name: Row i of kv_tiles lists 6 different tiles; each of their three tile coordinates differs from tile i's by at most one. `kv_count`: some tile uses all 6 listed tiles.
All inputs are finite; a program needn't handle non-finite values.
Results may differ from a plain program's by a relative error of at most 0.011.
Values may be sent and summed in bfloat16 or wider, within the bound.
No kernel may reach another device: no remote copies, remote signals or barrier semaphores. Data moves between devices by JAX's collectives and lax.ppermute only.
A program may use at most 192 MiB of HBM per device.

v0:
```python
import jax
import jax.numpy as jnp
from jax import lax
from jax.sharding import PartitionSpec as P

HD = 128
NH = 12
TF = 6
TH = 8
TW = 8
NB = 6
GH = 2


def extended(block, sides, width):
    for axis, dim in sides:
        count = lax.axis_size(axis)
        forward = [(i, i + 1) for i in range(count - 1)]
        backward = [(target, source) for source, target in forward]
        low = lax.ppermute(
            lax.slice_in_dim(block, block.shape[dim] - width, None, axis=dim), axis, forward
        )
        high = lax.ppermute(lax.slice_in_dim(block, 0, width, axis=dim), axis, backward)
        block = jnp.concatenate([low, block, high], axis=dim)
    return block


def local(modulated, mod_gate, w_qkv, w_out, kv_tiles, kv_count):
    tok_rows = modulated.shape[0]
    seq_count = lax.axis_size("seq")
    blk_count = lax.axis_size("blk")
    heads_local = NH // blk_count
    channels = heads_local * 3 * HD
    row_band = tok_rows // (seq_count * TW)
    projected = jnp.dot(
        modulated,
        lax.all_gather(w_qkv, "blk", axis=1, tiled=True),
        preferred_element_type=jnp.float32,
    ).astype(jnp.bfloat16)
    parcel = projected.reshape(row_band, seq_count, TW, blk_count, channels).transpose(
        1, 3, 0, 2, 4
    )
    parcel = parcel.reshape(seq_count * blk_count, row_band, TW, channels)
    strip = lax.all_to_all(parcel, ("seq", "blk"), split_axis=0, concat_axis=0, tiled=True)
    strip = strip.reshape(-1, TW, heads_local, 3, HD)
    strip_rows = strip.shape[0]
    layers = strip_rows // (GH * TH * TF)
    query_tiles_count = layers * GH
    tile_cells = TF * TH * TW
    queries = strip[:, :, :, 0, :]
    keyvals = strip[:, :, :, 1:, :]
    widened = extended(keyvals, (("seq", 1),), TW)
    query_heads = queries.reshape(layers, TF, GH, TH, TW, heads_local, HD)
    query_heads = query_heads.transpose(5, 0, 2, 1, 3, 4, 6).reshape(
        heads_local, query_tiles_count, tile_cells, HD
    )
    key_tiles = widened.reshape(layers, TF, GH, TH, 3, TW, heads_local, 2, HD)
    key_tiles = key_tiles.transpose(0, 2, 4, 1, 3, 5, 6, 7, 8).reshape(
        query_tiles_count * 3, tile_cells, heads_local, 2, HD
    )
    seq_index = lax.axis_index("seq")
    own_lists = lax.dynamic_index_in_dim(
        kv_tiles.reshape(query_tiles_count, seq_count, NB), seq_index, 1, keepdims=False
    )
    live_slots = lax.dynamic_index_in_dim(
        kv_count.reshape(query_tiles_count, seq_count), seq_index, 1, keepdims=False
    )
    slot_index = own_lists // seq_count * 3 + (own_lists % seq_count - seq_index + 1)
    chosen = jnp.take(key_tiles, slot_index.reshape(-1), axis=0)
    chosen = chosen.reshape(query_tiles_count, NB, tile_cells, heads_local, 2, HD)
    key_heads = chosen[:, :, :, :, 0, :].transpose(3, 0, 1, 2, 4)
    value_heads = chosen[:, :, :, :, 1, :].transpose(3, 0, 1, 2, 4)
    slot_open = (jnp.arange(NB, dtype=jnp.int32)[None, :] < live_slots[:, None])[:, None, :, None]
    score_scale = 1.0 / HD**0.5

    def attend(operands):
        query_head, key_head, value_head = operands
        scores = (
            jnp.einsum("qtd,qnsd->qtns", query_head, key_head, preferred_element_type=jnp.float32)
            * score_scale
        )
        scores = jnp.where(slot_open, scores, -jnp.inf)
        peak_score = jnp.max(scores, axis=(2, 3), keepdims=True)
        weights = jnp.exp(scores - peak_score)
        denom_sum = jnp.sum(weights, axis=(2, 3), keepdims=True)
        mixed = jnp.einsum(
            "qtns,qnsd->qtd",
            weights.astype(jnp.bfloat16),
            value_head,
            preferred_element_type=jnp.float32,
        )
        return (mixed / denom_sum[:, :, 0]).astype(jnp.bfloat16)

    attended = lax.map(attend, (query_heads, key_heads, value_heads))
    attended = attended.reshape(heads_local, layers, GH, TF, TH, TW, HD)
    result = attended.transpose(1, 3, 2, 4, 5, 0, 6).reshape(strip_rows, TW, heads_local * HD)
    head_width = heads_local * HD
    parcel_back = result.reshape(seq_count * blk_count, row_band, TW, head_width)
    arrived = lax.all_to_all(parcel_back, ("seq", "blk"), split_axis=0, concat_axis=0, tiled=True)
    arrived = arrived.reshape(seq_count, blk_count, row_band, TW, head_width).transpose(
        2, 0, 3, 1, 4
    )
    slab = arrived.reshape(tok_rows, NH * HD)
    return (
        jnp.dot(
            slab,
            lax.all_gather(w_out, "blk", axis=1, tiled=True),
            preferred_element_type=jnp.float32,
        )
        * mod_gate
    ).astype(jnp.bfloat16)


def solution(mesh):
    return jax.shard_map(
        local,
        mesh=mesh,
        in_specs=(
            P(("clip", "seq", "blk"), None),
            P("clip"),
            P(None, "blk"),
            P(None, "blk"),
            P("clip", None),
            P("clip"),
        ),
        out_specs=P(("clip", "seq", "blk"), None),
        check_vma=False,
    )
```

profile of v0, /device:TPU:1, one launch (start us, length us, event | category | flops | bytes accessed | tf_op | source)
XLA Modules:
  0.0 1030.8 jit_solution(8496969453207855809)
XLA Ops:
  6.5 0.7 all-gather.3.cloned.1.call-update
  7.3 334.4 %all-gather.3.cloned.1.call-done = bf16[3072,4608]{1,0:T(8,128)(2,1)} async-done(((bf16[3072,2304]{1,0:T(8,128)(2,1)}), bf16[3072,4608]{1,0:T(8,128)(2,1)}) %all-gather.3.cloned.1.call-update) | async-done | bytes 28311568 | tf_op jit(solution)/shard_map/all_gather | solution.py:37
  341.7 27.4 %convolution_convert_fusion = bf16[768,4608]{1,0:T(8,128)(2,1)S(1)} fusion(bf16[768,3072]{1,0:T(8,128)(2,1)} %param.8, bf16[3072,4608]{1,0:T(8,128)(2,1)} %all-gather.3.cloned.1.call-done), kind=kOutput, calls=%fused_computation.32 | convolution fusion | flops 21746810880 | bytes 40108032 | tf_op jit(solution)/shard_map/dot_general | solution.py:35
  369.1 0.7 copy.16
  369.8 159.9 %all_to_all.10 = bf16[16,12,8,2304]{3,2,1,0:T(8,128)(2,1)S(1)} all-to-all(bf16[16,12,8,2304]{3,2,1,0:T(8,128)(2,1)S(1)} %bitcast.119), channel_id=1, replica_groups=mesh['seq'=8,'blk'=2,'clip'=2] {'seq','blk'}, dimensions={0} | all-to-all | bytes 14155776 | tf_op jit(solution)/shard_map/all_to_all | solution.py:44
  529.8 2.9 copy-done.1
  532.7 3.0 slice.19
  535.7 1.3 collective-permute-start.1
  537.0 6.1 collective-permute-start
  543.8 2.1 slice.18
  545.9 2.1 copy.17
  548.0 90.9 %collective-permute-done.1 = bf16[192,8,6,2,128]{4,1,3,2,0:T(8,128)(2,1)} collective-permute-done((bf16[192,8,6,2,128]{4,1,3,2,0:T(8,128)(2,1)}, bf16[192,8,6,2,128]{4,1,3,2,0:T(8,128)(2,1)}, u32[]{:S(2)}, u32[]{:S(2)}) %collective-permute-start.1) | collective-permute-done | bytes 4718624 | tf_op jit(solution)/shard_map/ppermute | solution.py:23
  638.9 103.3 %collective-permute-done = bf16[192,8,6,2,128]{4,1,3,2,0:T(8,128)(2,1)} collective-permute-done((bf16[192,8,6,2,128]{4,1,3,2,0:T(8,128)(2,1)}, bf16[192,8,6,2,128]{4,1,3,2,0:T(8,128)(2,1)}, u32[]{:S(2)}, u32[]{:S(2)}) %collective-permute-start) | collective-permute-done | bytes 4718624 | tf_op jit(solution)/shard_map/ppermute | solution.py:20
  742.1 7.7 pad_maximum_fusion
  749.9 7.0 copy.19
  756.9 15.8 %gather_fusion = bf16[24,384,6,2,128]{4,1,3,2,0:T(8,128)(2,1)} fusion(bf16[12,384,6,2,128]{4,1,3,2,0:T(8,128)(2,1)} %bitcast.114, s32[1024]{0:T(1024)S(1)} %pad_clamp_fusion), kind=kCustom, calls=%fused_computation | custom fusion | bytes 56623200 | tf_op jit(solution)/shard_map/jit(_take)/gather | solution.py:69
  772.7 19.8 %copy_select_fusion = bf16[4,6,384,6,2,128]{5,2,1,0,3,4:T(8,128)(2,1)} fusion(bf16[4,6,384,6,2,128]{5,2,4,3,1,0:T(8,128)(2,1)} %bitcast.115, pred[4,6]{1,0:T(4,128)(4,1)S(1)} %compare_and_fusion), kind=kLoop, calls=%fused_computation.27 | loop fusion | flops 14155776 | bytes 56623128 | tf_op jit(solution)/shard_map/jit(_take)/select_n | solution.py:69
  792.6 22.3 %slice_bitcast_fusion = (bf16[6,4,6,384,128]{4,3,2,1,0:T(8,128)(2,1)}, bf16[6,4,6,384,128]{4,3,2,1,0:T(8,128)(2,1)}) fusion(bf16[4,6,384,6,2,128]{5,2,1,0,3,4:T(8,128)(2,1)} %copy_select_fusion), kind=kLoop, calls=%fused_computation.28 | loop fusion | bytes 56623104 | tf_op jit(solution)/shard_map/transpose | solution.py:72
  814.9 132.6 %while.11 = (s32[]{:T(128)}, bf16[6,4,384,128]{3,2,1,0:T(8,128)(2,1)}, bf16[6,4,384,128]{3,2,1,0:T(8,128)(2,1)}, bf16[6,4,6,384,128]{4,3,2,1,0:T(8,128)(2,1)}, b...) while((s32[]{:T(128)}, bf16[6,4,384,128]{3,2,1,0:T(8,128)(2,1)}, ...), condition=%wide.region_3.4_spmd.clone, body=%wide.region_0.3_spmd.clone.sunk | while | flops 1851257856 | bytes 104628448 | solution.py:94
  815.0 3.8 fusion.69
  818.8 5.0 copy-done
  823.9 3.0 fusion.70
  826.9 10.2 fusion.71
  837.1 3.8 fusion.69
  840.9 5.0 copy-done
  846.0 3.0 fusion.70
  849.0 10.2 fusion.71
  859.2 3.8 fusion.69
  863.0 5.0 copy-done
  868.1 3.0 fusion.70
  871.1 10.2 fusion.71
  881.3 3.8 fusion.69
  885.2 5.0 copy-done
  890.2 3.0 fusion.70
  893.2 10.2 fusion.71
  903.4 3.8 fusion.69
  907.3 5.0 copy-done
  912.3 3.0 fusion.70
  915.3 10.2 fusion.71
  925.5 3.8 fusion.69
  929.4 5.0 copy-done
  934.4 3.0 fusion.70
  937.4 10.2 fusion.71
  947.6 2.1 copy.21
  949.6 57.9 %all_to_all.11 = bf16[16,12,8,768]{3,2,1,0:T(8,128)(2,1)S(1)} all-to-all(bf16[16,12,8,768]{3,2,1,0:T(8,128)(2,1)S(1)} %bitcast.121), channel_id=1, replica_groups=mesh['seq'=8,'blk'=2,'clip'=2] {'seq','blk'}, dimensions={0} | all-to-all | bytes 4718592 | tf_op jit(solution)/shard_map/all_to_all | solution.py:99
  1007.5 3.2 copy.22
  1010.8 0.4 copy.27
  1011.2 12.7 %multiply_convert_fusion = bf16[768,3072]{1,0:T(8,128)(2,1)} fusion(bf16[768,1536]{1,0:T(8,128)(2,1)S(1)} %bitcast.127, bf16[1536,3072]{1,0:T(8,128)(2,1)} %all-gather.5.cloned.1.call-done, f32[3072]{0:T(1024)S(1)} %copy-done.4), kind=kOutput, calls=%fused_computation.31 | convolution fusion | flops 7252475904 | bytes 16527360 | tf_op jit(solution)/shard_map/dot_general | solution.py:105
  (33 shorter events, 1.2 us)
Async XLA Ops:
  6.5 335.1 %all-gather.3.cloned.1.call-start = ((), (), s32[]{:S(2)}) async-start(), calls=%async_computation.2 | async-start | bytes 42467328 | tf_op jit(solution)/shard_map/all_gather | solution.py:37
  7.3 1004.0 %all-gather.5.cloned.1.call-start = ((), (), s32[]{:S(2)}) async-start(), calls=%async_computation.3 | async-start | bytes 14155776 | tf_op jit(solution)/shard_map/all_gather | solution.py:107
  369.8 173.3 %copy-start.2 = (s32[32,6]{0,1:T(8,128)S(1)}, s32[32,6]{0,1:T(8,128)}, u32[]{:S(2)}) copy-start(s32[32,6]{0,1:T(8,128)} %param.12) | copy-start | bytes 2308
  369.8 173.6 %copy-start.3 = (s32[32]{0:T(128)S(1)}, s32[32]{0:T(128)}, u32[]{:S(2)}) copy-start(s32[32]{0:T(128)} %param.13) | copy-start | bytes 388
  529.8 2.9 copy-start.1
  535.7 103.2 %collective-permute-start.1 = (bf16[192,8,6,2,128]{4,1,3,2,0:T(8,128)(2,1)}, bf16[192,8,6,2,128]{4,1,3,2,0:T(8,128)(2,1)}, u32[]{:S(2)}, u32[]{:S(2)}) collective-permute-start(bf16[192,8,6,2,128]{4,1,3,2,0:T(8,128)(2,1)} %slice.19), channel_id=1, source_target_pairs={{4,0},{8,4},{12,8},{16,12},{20,16},{24,20},{28,24},{5,1},{9,5},{13... | collective-permute-start | bytes 14155784 | tf_op jit(solution)/shard_map/ppermute | solution.py:23
  537.0 205.2 %collective-permute-start = (bf16[192,8,6,2,128]{4,1,3,2,0:T(8,128)(2,1)}, bf16[192,8,6,2,128]{4,1,3,2,0:T(8,128)(2,1)}, u32[]{:S(2)}, u32[]{:S(2)}) collective-permute-start(bf16[192,8,6,2,128]{4,1,3,2,0:T(8,128)(2,1)} %slice.19), channel_id=1, source_target_pairs={{0,4},{4,8},{8,12},{12,16},{16,20},{20,24},{24,28},{1,5},{5,9},{9,... | collective-permute-start | bytes 14155784 | tf_op jit(solution)/shard_map/ppermute | solution.py:20
  818.8 5.1 copy-start
  840.9 5.1 copy-start
  863.0 5.1 copy-start
  885.1 5.1 copy-start
  907.3 5.1 copy-start
  929.4 5.1 copy-start
  947.6 63.7 %copy-start.4 = (f32[3072]{0:T(1024)S(1)}, f32[3072]{0:T(1024)}, u32[]{:S(2)}) copy-start(f32[3072]{0:T(1024)} %param.9) | copy-start | bytes 36868
Sparse Core Ops, SparseCore 0:
  8.9 332.7 all-gather.2
  543.2 117.6 all-gather.4
where the time goes:
time: 1030 us
  waiting for transfers between devices  529 us (51%)
  blocking collectives  218 us (21%)
  matrix products  124 us (12%)
  local copies, waits for them, and re-layouts  92.6 us (9%)
  other arithmetic  46 us (4%)
  between operations  13.5 us (1%)
    all_gather x1, waiting for transfers between devices, local(): lax.all_gather(w_qkv, 'blk', axis=1, tiled=True)  334 us
    all_to_all x1, blocking collectives, local(): lax.all_to_all(parcel, ('seq', 'blk'), split_axis=0, concat_axis=0, tiled...  160 us
    ppermute x1, waiting for transfers between devices, extended(): lax.ppermute(lax.slice_in_dim(block, block.shape[dim] - width, None, axis...  103 us
    ppermute x1, waiting for transfers between devices, extended(): lax.ppermute(lax.slice_in_dim(block, 0, width, axis=dim), axis, backward)  90.9 us
    dot_general x6, matrix products, attend(): jnp.einsum('qtns,qnsd->qtd', weights.astype(jnp.bfloat16), value_head, pr...  61 us
    all_to_all x1, blocking collectives, local(): lax.all_to_all(parcel_back, ('seq', 'blk'), split_axis=0, concat_axis=0,...  57.9 us
    while x12, local copies, waits for them, and re-layouts  30.3 us
    dot_general x1, matrix products, local(): jnp.dot(modulated, lax.all_gather(w_qkv, 'blk', axis=1, tiled=True), pref...  27.4 us
  transfers between devices with their start and end apart: 4, of which 3 were waited for; matrix products, arithmetic and copies ran while one was open for 18% of the time, Pallas kernels for 0%

commit v1 on v0

v1 whole, which is shorter than its diff:
```python
import functools
import math

import jax
import jax.numpy as jnp
from jax import lax
from jax.experimental import pallas as pl
from jax.experimental.pallas import tpu as pltpu
from jax.sharding import PartitionSpec as P

HD = 128
NH = 12
TF = 6
TH = 8
TW = 8
NB = 6
GH = 2
CELLS = TF * TH * TW
AXES = ("seq", "blk", "clip")
GROUPS = 4
HPD = NH // GROUPS
EXP2_SCALE = math.log2(math.e) / math.sqrt(HD)
MIB = 1 << 20


def permuted(array, seq_count, target):
    pairs = []
    for seq in range(seq_count):
        for blk in range(2):
            for clip in range(2):
                goal = target(seq // 2, seq % 2, blk, clip)
                if goal is not None:
                    strip, half, blk_to, clip_to = goal
                    pairs.append(
                        ((seq * 2 + blk) * 2 + clip, ((strip * 2 + half) * 2 + blk_to) * 2 + clip_to)
                    )
    return lax.ppermute(array, AXES, pairs)


def projection_body(first, place, *refs):
    pieces, weight = refs[:4], refs[4]
    skip = 5 if first else 5 + 3 * HPD
    outs = refs[skip : skip + 3 * HPD]
    tokens, columns, blocks, token_sem, weight_sem, out_sem = refs[skip + 3 * HPD :]
    piece_rows = pieces[0].shape[0]
    part = piece_rows // 2
    rows = 4 * piece_rows
    loads = []
    for i in range(4):
        start = pl.multiple_of(place[i] * piece_rows, piece_rows)
        loads.append(
            pltpu.make_async_copy(
                pieces[i], tokens.at[pl.ds(start, piece_rows)], token_sem.at[i]
            )
        )
    width = 3 * HD
    streams = []
    for head in range(HPD):
        start = pl.multiple_of((place[5] * HPD + head) * width, HD)
        streams.append(
            pltpu.make_async_copy(
                weight.at[:, pl.ds(start, width)], columns.at[head], weight_sem.at[head]
            )
        )
    for copy in loads:
        copy.start()
    for copy in streams:
        copy.start()
    for copy in loads:
        copy.wait()
    row_start = pl.multiple_of(place[4] * (4 * part), 4 * part)
    stores = []
    for head in range(HPD):
        streams[head].wait()
        total = jnp.dot(tokens[...], columns[head], preferred_element_type=jnp.float32)
        for kind in range(3):
            for column in range(2):
                block = jnp.concatenate(
                    [
                        total[
                            i * piece_rows + column * part : i * piece_rows + (column + 1) * part,
                            kind * HD : (kind + 1) * HD,
                        ]
                        for i in range(4)
                    ],
                    axis=0,
                )
                blocks[head, kind, column] = block.astype(jnp.bfloat16)
                if kind == 0:
                    target = outs[head * 3].at[column, pl.ds(row_start, 4 * part)]
                else:
                    target = outs[head * 3 + 1 + column].at[kind - 1, pl.ds(row_start, 4 * part)]
                copy = pltpu.make_async_copy(
                    blocks.at[head, kind, column],
                    target,
                    out_sem.at[(head * 3 + kind) * 2 + column],
                )
                copy.start()
                stores.append(copy)
    for copy in stores:
        copy.wait()


def project(place, pieces, weight, before, strip_tokens):
    piece_rows, depth = pieces[0].shape
    first = before is None
    out_shape = [jax.ShapeDtypeStruct((2, strip_tokens, HD), jnp.bfloat16)] * (3 * HPD)
    operands = list(pieces) + [weight] + ([] if first else list(before))
    anywhere = pl.BlockSpec(memory_space=pl.ANY)
    return pl.pallas_call(
        functools.partial(projection_body, first),
        out_shape=out_shape,
        in_specs=[pl.BlockSpec(memory_space=pltpu.SMEM)] + [anywhere] * len(operands),
        out_specs=[anywhere] * len(out_shape),
        scratch_shapes=[
            pltpu.VMEM((4 * piece_rows, depth), jnp.bfloat16),
            pltpu.VMEM((HPD, depth, 3 * HD), jnp.bfloat16),
            pltpu.VMEM((HPD, 3, 2, 2 * piece_rows, HD), jnp.bfloat16),
            pltpu.SemaphoreType.DMA((4,)),
            pltpu.SemaphoreType.DMA((HPD,)),
            pltpu.SemaphoreType.DMA((6 * HPD,)),
        ],
        input_output_aliases={} if first else {6 + i: i for i in range(3 * HPD)},
        compiler_params=pltpu.CompilerParams(vmem_limit_bytes=40 * MIB),
        cost_estimate=pl.CostEstimate(
            flops=8 * piece_rows * depth * 3 * HD * HPD,
            bytes_accessed=2 * depth * (4 * piece_rows + 3 * HD * HPD),
            transcendentals=0,
        ),
    )(place, *operands)


def attention_body(
    layers, slots, counts, query, left, own0, own1, right, out, keyvals, scores, peak, denom, mixed, sems
):
    copies = []
    for i, source in enumerate((left, own0, own1, right)):
        copy = pltpu.make_async_copy(source, keyvals.at[i], sems.at[i])
        copy.start()
        copies.append(copy)
    for copy in copies:
        copy.wait()

    def one_tile(tile, carry):
        column = tile // (layers * GH)
        layer = tile // GH % layers
        half = tile % GH
        count = counts[tile]
        queries = query[column, layer, :, half].reshape(CELLS, HD)
        peak[...] = jnp.full(peak.shape, -jnp.inf, jnp.float32)
        denom[...] = jnp.zeros(denom.shape, jnp.float32)
        mixed[...] = jnp.zeros(mixed.shape, jnp.float32)

        def score(slot, inner):
            spot = slots[tile * NB + slot]
            keys = keyvals[spot // (layers * GH), 0, spot // GH % layers, :, spot % GH]
            found = lax.dot_general(
                queries,
                keys.reshape(CELLS, HD),
                (((1,), (1,)), ((), ())),
                preferred_element_type=jnp.float32,
            )
            scores[slot] = found
            top = peak[...]
            for lane in range(CELLS // HD):
                top = jnp.maximum(top, found[:, lane * HD : (lane + 1) * HD])
            peak[...] = top
            return inner

        lax.fori_loop(0, count, score, 0)
        offset = jnp.max(peak[...], axis=1, keepdims=True) * EXP2_SCALE

        def mix(slot, inner):
            spot = slots[tile * NB + slot]
            values = keyvals[spot // (layers * GH), 1, spot // GH % layers, :, spot % GH]
            weights = jnp.exp2(scores[slot] * EXP2_SCALE - offset)
            total = denom[...]
            for lane in range(CELLS // HD):
                total = total + weights[:, lane * HD : (lane + 1) * HD]
            denom[...] = total
            mixed[...] += jnp.dot(
                weights.astype(jnp.bfloat16),
                values.reshape(CELLS, HD),
                preferred_element_type=jnp.float32,
            )
            return inner

        lax.fori_loop(0, count, mix, 0)
        result = mixed[...] / jnp.sum(denom[...], axis=1, keepdims=True)
        out[column, layer, :, half] = result.astype(jnp.bfloat16).reshape(TF, TH * TW, HD)
        return carry

    lax.fori_loop(0, 2 * layers * GH, one_tile, 0)


def attend(slots, counts, query, left, own0, own1, right):
    layers = query.shape[1] // (TF * GH * TH * TW)
    shape = (2, layers, TF, GH, TH * TW, HD)
    smem = pl.BlockSpec(memory_space=pltpu.SMEM)
    vmem = pl.BlockSpec(memory_space=pltpu.VMEM)
    anywhere = pl.BlockSpec(memory_space=pl.ANY)
    out = pl.pallas_call(
        functools.partial(attention_body, layers),
        out_shape=jax.ShapeDtypeStruct(shape, jnp.bfloat16),
        in_specs=[smem, smem, vmem] + [anywhere] * 4,
        out_specs=vmem,
        scratch_shapes=[
            pltpu.VMEM((4,) + shape, jnp.bfloat16),
            pltpu.VMEM((NB, CELLS, CELLS), jnp.float32),
            pltpu.VMEM((CELLS, HD), jnp.float32),
            pltpu.VMEM((CELLS, HD), jnp.float32),
            pltpu.VMEM((CELLS, HD), jnp.float32),
            pltpu.SemaphoreType.DMA((4,)),
        ],
        compiler_params=pltpu.CompilerParams(vmem_limit_bytes=40 * MIB),
        cost_estimate=pl.CostEstimate(
            flops=2 * layers * GH * NB * CELLS * CELLS * HD * 2,
            bytes_accessed=12 * layers * GH * CELLS * HD * 2,
            transcendentals=2 * layers * GH * NB * CELLS * CELLS // 2,
        ),
    )(slots, counts, *[a.reshape(shape) for a in (query, left, own0, own1, right)])
    return out.reshape(query.shape)


def output_body(rounds, rows, strips, *refs):
    pieces = refs[: rounds * HPD]
    weight, gate, out, mixed, sems = refs[rounds * HPD :]
    part = rows * TW

    @pl.when(pl.program_id(0) == 0)
    def _():
        copies = []
        for i in range(rounds):
            for head in range(HPD):
                for group in range(GROUPS):
                    copy = pltpu.make_async_copy(
                        pieces[i * HPD + head].at[group],
                        mixed.at[
                            pl.ds(i * 2 * part, 2 * part),
                            pl.ds((head * GROUPS + group) * HD, HD),
                        ],
                        sems.at[i],
                    )
                    copy.start()
                    copies.append(copy)
        for copy in copies:
            copy.wait()

    product = (
        jnp.dot(mixed[...], weight[...], preferred_element_type=jnp.float32) * gate[...]
    )
    for i in range(rounds):
        strip = strips[i]
        for row in range(rows):
            base = i * 2 * part + row * TW
            both = jnp.concatenate(
                [product[base : base + TW], product[base + part : base + part + TW]], axis=0
            )
            out[row, strip] = both.astype(jnp.bfloat16)


def project_out(strips, pieces, weight, gate, rows):
    rounds = len(pieces) // HPD
    depth, width = weight.shape
    step = 512
    anywhere = pl.BlockSpec(memory_space=pl.ANY)
    return pl.pallas_call(
        lambda strips_ref, *refs: output_body(rounds, rows, strips_ref, *refs),
        out_shape=jax.ShapeDtypeStruct((rows, rounds, 2 * TW, width), jnp.bfloat16),
        grid=(width // step,),
        in_specs=[pl.BlockSpec(memory_space=pltpu.SMEM)]
        + [anywhere] * len(pieces)
        + [
            pl.BlockSpec((depth, step), lambda n: (0, n)),
            pl.BlockSpec((1, step), lambda n: (0, n)),
        ],
        out_specs=pl.BlockSpec((rows, rounds, 2 * TW, step), lambda n: (0, 0, 0, n)),
        scratch_shapes=[
            pltpu.VMEM((rounds * rows * 2 * TW, depth), jnp.bfloat16),
            pltpu.SemaphoreType.DMA((rounds,)),
        ],
        compiler_params=pltpu.CompilerParams(vmem_limit_bytes=40 * MIB),
    )(strips, *pieces, weight, gate)


def local(modulated, mod_gate, w_qkv, w_out, kv_tiles, kv_count):
    tok_rows, depth = modulated.shape
    seq_count = lax.axis_size("seq")
    rounds = seq_count // 2
    rows = tok_rows // (seq_count * TW)
    part = rows * TW
    strip_tokens = rounds * 4 * part
    layers = strip_tokens // (TF * GH * TH * TW)
    seq_index = lax.axis_index("seq")
    strip, half = seq_index // 2, seq_index % 2
    blk, clip = lax.axis_index("blk"), lax.axis_index("clip")

    def swap(array, over_blk, over_clip):
        return permuted(
            array, seq_count, lambda s, h, b, c: (s, h, b ^ over_blk, c ^ over_clip)
        )

    def regroup(array, distance):
        return permuted(array, seq_count, lambda s, h, b, c: (s ^ distance, c, b, h))

    by_strip = modulated.reshape(rows, rounds, 2, TW, depth)
    pieces = []
    for i in range(rounds):
        sent = lax.dynamic_index_in_dim(by_strip, strip ^ i, 1, keepdims=False)
        sent = sent.transpose(1, 0, 2, 3).reshape(2 * part, depth)
        pieces.append(regroup(sent, i))
    quads = []
    for piece in pieces:
        across = swap(piece, 1, 0)
        quads.append((piece, across, swap(piece, 0, 1), swap(across, 0, 1)))

    lists = jnp.concatenate([kv_tiles, kv_count[:, None]], axis=1)
    lists = regroup(lists, 0).reshape(layers * GH, seq_count, NB + 1)
    lists = lax.dynamic_slice_in_dim(lists, strip * 2, 2, axis=1).transpose(1, 0, 2)
    lists = lists.reshape(2 * layers * GH, NB + 1)
    counts = lists[:, NB]
    tiles = lists[:, :NB]
    slots = (tiles % seq_count - strip * 2 + 1) * (layers * GH) + tiles // seq_count
    slots = slots.reshape(-1)

    placed = None
    for i, quad in enumerate(quads):
        place = jnp.stack(
            [
                clip * 2 + blk,
                clip * 2 + 1 - blk,
                (1 - clip) * 2 + blk,
                (1 - clip) * 2 + 1 - blk,
                strip ^ i,
                clip,
            ]
        ).astype(jnp.int32)
        placed = project(place, quad, w_qkv, placed, strip_tokens)

    w_half = w_out.shape[0] // 2
    w_sent = lax.dynamic_slice_in_dim(w_out, clip * w_half, w_half, axis=0)
    w_sent, _ = lax.optimization_barrier((w_sent, quads[-1][1]))
    w_got = swap(w_sent, 1, 0)
    w_also = swap(w_got, 0, 1)
    w_other = jnp.where(
        clip == 0,
        jnp.concatenate([w_got, w_also], axis=0),
        jnp.concatenate([w_also, w_got], axis=0),
    )
    w_full = jnp.where(
        blk == 0,
        jnp.concatenate([w_out, w_other], axis=1),
        jnp.concatenate([w_other, w_out], axis=1),
    )
    w_full = w_full.reshape(2, 2, HPD, HD, -1)
    heads = []
    for head in range(HPD):
        for over_blk, over_clip in ((0, 0), (0, 1), (1, 0), (1, 1)):
            block = lax.dynamic_index_in_dim(w_full, blk ^ over_blk, 0, keepdims=False)
            heads.append(lax.dynamic_index_in_dim(block, half ^ over_clip, 0, keepdims=False)[head])
    w_rows = jnp.concatenate(heads, axis=0)

    returned = [[None] * HPD for _ in range(rounds)]
    for head in range(HPD):
        query, own0, own1 = placed[head * 3 : head * 3 + 3]
        left = permuted(
            own1, seq_count, lambda s, h, b, c: (s + 1, h, b, c) if s + 1 < rounds else None
        )
        right = permuted(own0, seq_count, lambda s, h, b, c: (s - 1, h, b, c) if s else None)
        result = attend(slots, counts, query, left, own0, own1, right)
        result = result.reshape(2, rounds, 2, 2, part, HD)

        def towards(over_blk, over_clip):
            some = lax.dynamic_index_in_dim(result, clip ^ over_clip, 2, keepdims=False)
            return lax.dynamic_index_in_dim(some, blk ^ over_blk, 2, keepdims=False)

        group = jnp.stack(
            [
                towards(0, 0),
                swap(towards(0, 1), 0, 1),
                swap(towards(1, 0), 1, 0),
                swap(towards(1, 1), 1, 1),
            ]
        )
        for i in range(rounds):
            sent = lax.dynamic_index_in_dim(group, strip ^ i, 2, keepdims=False)
            returned[i][head] = regroup(sent.reshape(GROUPS, 2 * part, HD), i)

    strips = jnp.stack([strip ^ i for i in range(rounds)]).astype(jnp.int32)
    flat = [returned[i][head] for i in range(rounds) for head in range(HPD)]
    out = project_out(strips, flat, w_rows, mod_gate.reshape(1, -1), rows)
    return out.reshape(tok_rows, -1)


def solution(mesh):
    return jax.shard_map(
        local,
        mesh=mesh,
        in_specs=(
            P(("clip", "seq", "blk"), None),
            P("clip"),
            P(None, "blk"),
            P(None, "blk"),
            P("clip", None),
            P("clip"),
        ),
        out_specs=P(("clip", "seq", "blk"), None),
        check_vma=False,
    )
```

time: 1030 us -> 425 us (0.41)
  the two profiles are of different devices: /device:TPU:1 before, /device:TPU:11 now
where the time goes in v1:
time: 425 us; the launch traced here: 419 us
  waiting for transfers between devices  199 us (47%)
  Pallas kernels  130 us (31%)
  starting transfers between devices  70 us (16%)
  local copies, waits for them, and re-layouts  11.1 us (3%)
  other arithmetic  7.92 us (2%)
    ppermute x46, waiting for transfers between devices, permuted(): return lax.ppermute(array, AXES, pairs)  199 us
    ppermute x46, starting transfers between devices, permuted(): return lax.ppermute(array, AXES, pairs)  70 us
    pallas_call x3, Pallas kernels, attend(): pl.pallas_call(functools.partial(attention_body, layers), out_shape=jax.S...  60.3 us
    pallas_call x4, Pallas kernels, project(): pl.pallas_call(functools.partial(projection_body, first), out_shape=out_s...  58.4 us
    pallas_call x1, Pallas kernels, project_out(): pl.pallas_call(lambda strips_ref, *refs: output_body(rounds, rows, strips...  10.9 us
  transfers between devices with their start and end apart: 46, of which 17 were waited for; matrix products, arithmetic and copies ran while one was open for 3% of the time, Pallas kernels for 28%

profile of v1, /device:TPU:11, one launch (start us, length us, event | category | flops | bytes accessed | tf_op | source)
XLA Modules:
  0.0 418.9 jit_solution(13172134200313037065)
XLA Ops:
  0.0 2.7 constant_dynamic-slice_fusion.25
  2.8 2.9 collective-permute-start.1
  5.8 1.9 collective-permute-start.9
  7.8 3.7 collective-permute-start.13
  11.7 46.7 %collective-permute-done.1.refs_0_ = bf16[192,3072]{1,0:T(8,128)(2,1)} collective-permute-done((bf16[192,3072]{1,0:T(8,128)(2,1)S(1)}, bf16[192,3072]{1,0:T(8,128)(2,1)}, u32[]{:S(2)}, u32[]{:S(2)}) %collective-permute-start.1) | collective-permute-done | bytes 1179680 | tf_op jit(solution)/shard_map/ppermute | solution.py:37
  61.2 45.8 %collective-permute-done.5.refs_0_ = bf16[192,3072]{1,0:T(8,128)(2,1)} collective-permute-done((bf16[192,3072]{1,0:T(8,128)(2,1)S(1)}, bf16[192,3072]{1,0:T(8,128)(2,1)}, u32[]{:S(2)}, u32[]{:S(2)}) %collective-permute-start.5) | collective-permute-done | bytes 1179680 | tf_op jit(solution)/shard_map/ppermute | solution.py:37
  107.7 4.1 collective-permute-done.10.refs_1_
  111.9 25.3 %collective-permute-done.14.refs_1_ = bf16[192,3072]{1,0:T(8,128)(2,1)} collective-permute-done((bf16[192,3072]{1,0:T(8,128)(2,1)}, bf16[192,3072]{1,0:T(8,128)(2,1)}, u32[]{:S(2)}, u32[]{:S(2)}) %collective-permute-start.14) | collective-permute-done | bytes 1179680 | tf_op jit(solution)/shard_map/ppermute | solution.py:37
  137.5 24.3 %collective-permute-done.6.refs_1_ = bf16[192,3072]{1,0:T(8,128)(2,1)} collective-permute-done((bf16[192,3072]{1,0:T(8,128)(2,1)}, bf16[192,3072]{1,0:T(8,128)(2,1)}, u32[]{:S(2)}, u32[]{:S(2)}) %collective-permute-start.6) | collective-permute-done | bytes 1179680 | tf_op jit(solution)/shard_map/ppermute | solution.py:37
  162.3 2.1 constant_dynamic-slice_fusion
  165.6 15.4 %shard_map.64 = (bf16[2,1536,128]{2,1,0:T(8,128)(2,1)S(1)}, bf16[2,1536,128]{2,1,0:T(8,128)(2,1)S(1)}, bf16[2,1536,128]{2,1,0:T(8,128)(2,1)S(1)}, bf16[2,1536,12...) custom-call(s32[6]{0:T(128)S(1)} %stack.119.place, ...), custom_call_target="tpu_custom_call" | custom-call | flops 5435817984 | bytes 11796480 | tf_op jit(solution)/shard_map/pallas_call | solution.py:110
  181.0 15.5 %shard_map.65 = (bf16[2,1536,128]{2,1,0:T(8,128)(2,1)S(1)}, bf16[2,1536,128]{2,1,0:T(8,128)(2,1)S(1)}, bf16[2,1536,128]{2,1,0:T(8,128)(2,1)S(1)}, bf16[2,1536,12...) custom-call(s32[6]{0:T(128)S(1)} %stack.118.place, ...), custom_call_target="tpu_custom_call", output_to_operand_aliasing={{0}: (6, {}), {1}: (7, {}), {2}: (8, {}), {3}: (9, {}), {4}... | custom-call | flops 5435817984 | bytes 11796480 | tf_op jit(solution)/shard_map/pallas_call | solution.py:110
  196.5 13.7 %shard_map.66 = (bf16[2,1536,128]{2,1,0:T(8,128)(2,1)S(1)}, bf16[2,1536,128]{2,1,0:T(8,128)(2,1)S(1)}, bf16[2,1536,128]{2,1,0:T(8,128)(2,1)S(1)}, bf16[2,1536,12...) custom-call(s32[6]{0:T(128)S(1)} %stack.117.place, ...), custom_call_target="tpu_custom_call", output_to_operand_aliasing={{0}: (6, {}), {1}: (7, {}), {2}: (8, {}), {3}: (9, {}), {4}... | custom-call | flops 5435817984 | bytes 11796480 | tf_op jit(solution)/shard_map/pallas_call | solution.py:110
  210.2 13.9 %shard_map.67 = (bf16[2,1536,128]{2,1,0:T(8,128)(2,1)S(1)}, bf16[2,1536,128]{2,1,0:T(8,128)(2,1)S(1)}, bf16[2,1536,128]{2,1,0:T(8,128)(2,1)S(1)}, bf16[2,1536,12...) custom-call(s32[6]{0:T(128)S(1)} %stack.116.place, ...), custom_call_target="tpu_custom_call", output_to_operand_aliasing={{0}: (6, {}), {1}: (7, {}), {2}: (8, {}), {3}: (9, {}), {4}... | custom-call | flops 5435817984 | bytes 11796480 | tf_op jit(solution)/shard_map/pallas_call | solution.py:110
  226.8 3.0 collective-permute-start.17
  229.8 3.2 collective-permute-start.18
  233.7 1.9 collective-permute-start
  235.6 2.1 collective-permute-start.29
  239.0 2.8 collective-permute-start.30
  242.2 5.7 %collective-permute-done.17 = bf16[2,1536,128]{2,1,0:T(8,128)(2,1)} collective-permute-done((bf16[2,1536,128]{2,1,0:T(8,128)(2,1)S(1)}, bf16[2,1536,128]{2,1,0:T(8,128)(2,1)}, u32[]{:S(2)}, u32[]{:S(2)}) %collective-permute-start.17) | collective-permute-done | bytes 786464 | tf_op jit(solution)/shard_map/ppermute | solution.py:37
  247.9 3.0 collective-permute-start.23
  250.9 3.2 collective-permute-start.24
  254.4 20.0 %shard_map.68 = bf16[2,2,6,2,64,128]{5,4,3,2,1,0:T(8,128)(2,1)S(1)} custom-call(s32[48]{0:T(128)S(1)} %reshape.193.slots, s32[8]{0:T(128)S(1)} %slice_reduce_fusion.counts, bf16[2,2,6,2,64,128]{5,4,3,2,1,0:T(8,128)(2,1)S(1)} %bitcast.163, bf16[2,2,6,2,64,128]{5,4,3,2,1,0:T(8,128)(2,1)} %bitcast.27.left, bf16[2,2,6,2,64,128]{5,4,3,2,1,0:T(8,128)(2,1)S(1)} %bitcast.164, ...), custom_call_target="tpu_custom_call" | custom-call | flops 1811939328 | bytes 4718592 | tf_op jit(solution)/shard_map/pallas_call | solution.py:202
  274.5 3.1 collective-permute-start.21
  279.0 20.4 %shard_map.70 = bf16[2,2,6,2,64,128]{5,4,3,2,1,0:T(8,128)(2,1)S(1)} custom-call(s32[48]{0:T(128)S(1)} %reshape.193.slots, s32[8]{0:T(128)S(1)} %slice_reduce_fusion.counts, bf16[2,2,6,2,64,128]{5,4,3,2,1,0:T(8,128)(2,1)S(1)} %bitcast.169, bf16[2,2,6,2,64,128]{5,4,3,2,1,0:T(8,128)(2,1)} %bitcast.55.left, bf16[2,2,6,2,64,128]{5,4,3,2,1,0:T(8,128)(2,1)} %bitcast.56.own0, ...), custom_call_target="tpu_custom_call" | custom-call | flops 1811939328 | bytes 4718592 | tf_op jit(solution)/shard_map/pallas_call | solution.py:202
  299.8 1.4 collective-permute-start.33
  301.2 20.0 %shard_map.69 = bf16[2,2,6,2,64,128]{5,4,3,2,1,0:T(8,128)(2,1)S(1)} custom-call(s32[48]{0:T(128)S(1)} %reshape.193.slots, s32[8]{0:T(128)S(1)} %slice_reduce_fusion.counts, bf16[2,2,6,2,64,128]{5,4,3,2,1,0:T(8,128)(2,1)S(1)} %bitcast.166, bf16[2,2,6,2,64,128]{5,4,3,2,1,0:T(8,128)(2,1)} %bitcast.41.left, bf16[2,2,6,2,64,128]{5,4,3,2,1,0:T(8,128)(2,1)S(1)} %bitcast.167, ...), custom_call_target="tpu_custom_call" | custom-call | flops 1811939328 | bytes 4718592 | tf_op jit(solution)/shard_map/pallas_call | solution.py:202
  324.0 3.8 collective-permute-done.32
  329.1 1.9 collective-permute-start.22
  331.2 1.4 collective-permute-done.27
  332.6 3.6 collective-permute-done.26
  336.4 1.9 collective-permute-start.28
  338.4 3.6 collective-permute-start.34
  342.0 2.3 collective-permute-start.35
  344.7 5.0 %maximum_select_fusion.1 = bf16[1536,1536]{1,0:T(8,128)(2,1)S(1)} fusion(bf16[768,1536]{1,0:T(8,128)(2,1)} %collective-permute-done.45, bf16[768,1536]{1,0:T(8,128)(2,1)} %collective-permute-done.44, pred[]{:T(512)S(6)} %eq.11), kind=kLoop, calls=%fused_computation.1 | loop fusion | flops 21233664 | bytes 9437185 | tf_op jit(solution)/shard_map/jit(_where)/select_n | solution.py:345
  349.7 2.5 maximum_select_fusion
  353.0 2.3 collective-permute-start.37
  355.4 7.5 %collective-permute-start.38 = (bf16[4,192,128]{2,1,0:T(8,128)(2,1)S(1)}, bf16[4,192,128]{2,1,0:T(8,128)(2,1)S(1)}, u32[]{:S(2)}, u32[]{:S(2)}) collective-permute-start(bf16[4,192,128]{2,1,0:T(8,128)(2,1)S(1)} %bitcast.187), channel_id=1, source_target_pairs={{0,16},{1,20},{2,18},{3,22},{4,17},{5,21},{6,19},{7,23},{8,24},{9,... | collective-permute-start | bytes 589832 | tf_op jit(solution)/shard_map/ppermute | solution.py:37
  363.1 3.5 collective-permute-start.40
  366.6 3.6 collective-permute-start.42
  370.2 13.7 %collective-permute-done.38.refs_6_ = bf16[4,192,128]{2,1,0:T(8,128)(2,1)S(1)} collective-permute-done((bf16[4,192,128]{2,1,0:T(8,128)(2,1)S(1)}, bf16[4,192,128]{2,1,0:T(8,128)(2,1)S(1)}, u32[]{:S(2)}, u32[]{:S(2)}) %collective-permute-start.38) | collective-permute-done | bytes 196640 | tf_op jit(solution)/shard_map/ppermute | solution.py:37
  383.9 1.5 collective-permute-start.43
  385.4 2.6 collective-permute-done.39.refs_7_
  388.1 6.3 %collective-permute-done.40.refs_8_ = bf16[4,192,128]{2,1,0:T(8,128)(2,1)S(1)} collective-permute-done((bf16[4,192,128]{2,1,0:T(8,128)(2,1)S(1)}, bf16[4,192,128]{2,1,0:T(8,128)(2,1)S(1)}, u32[]{:S(2)}, u32[]{:S(2)}) %collective-permute-start.40) | collective-permute-done | bytes 196640 | tf_op jit(solution)/shard_map/ppermute | solution.py:37
  394.4 8.0 %collective-permute-done.41.refs_9_ = bf16[4,192,128]{2,1,0:T(8,128)(2,1)S(1)} collective-permute-done((bf16[4,192,128]{2,1,0:T(8,128)(2,1)S(1)}, bf16[4,192,128]{2,1,0:T(8,128)(2,1)S(1)}, u32[]{:S(2)}, u32[]{:S(2)}) %collective-permute-start.41) | collective-permute-done | bytes 196640 | tf_op jit(solution)/shard_map/ppermute | solution.py:37
  402.4 3.3 collective-permute-done.42.refs_10_
  405.7 2.1 collective-permute-done.43.refs_11_
  407.8 10.9 %shard_map.71 = bf16[12,4,16,3072]{3,2,1,0:T(8,128)(2,1)} custom-call(s32[4]{0:T(128)S(1)} %pad_add_fusion.1.strips_ref, bf16[4,192,128]{2,1,0:T(8,128)(2,1)S(1)} %collective-permute-done.22.refs_0_, bf16[4,192,128]{2,1,0:T(8,128)(2,1)S(1)} %collective-permute-done.28.refs_1_, bf16[4,192,128]{2,1,0:T(8,128)(2,1)S(1)} %collective-permute-done.34.refs_2_, ...), custom_call_target="tpu_custom_call" | custom-call | tf_op jit(solution)/shard_map/pallas_call | solution.py:267
  (139 shorter events, 18.9 us)
Async XLA Ops:
  2.8 55.6 %collective-permute-start.1 = (bf16[192,3072]{1,0:T(8,128)(2,1)S(1)}, bf16[192,3072]{1,0:T(8,128)(2,1)}, u32[]{:S(2)}, u32[]{:S(2)}) collective-permute-start(bf16[192,3072]{1,0:T(8,128)(2,1)S(1)} %bitcast.182), channel_id=1, source_target_pairs={{0,24},{1,28},{2,26},{3,30},{4,25},{5,29},{6,27},{7,31},{8,16},{9,... | collective-permute-start | bytes 3538952 | tf_op jit(solution)/shard_map/ppermute | solution.py:37
  5.8 53.9 %collective-permute-start.9 = (bf16[192,3072]{1,0:T(8,128)(2,1)S(1)}, bf16[192,3072]{1,0:T(8,128)(2,1)S(1)}, u32[]{:S(2)}, u32[]{:S(2)}) collective-permute-start(bf16[192,3072]{1,0:T(8,128)(2,1)S(1)} %bitcast.181), channel_id=1, source_target_pairs={{0,8},{1,12},{2,10},{3,14},{4,9},{5,13},{6,11},{7,15},{8,0},{9,4},... | collective-permute-start | bytes 3538952 | tf_op jit(solution)/shard_map/ppermute | solution.py:37
  7.8 52.2 %collective-permute-start.13 = (bf16[192,3072]{1,0:T(8,128)(2,1)S(1)}, bf16[192,3072]{1,0:T(8,128)(2,1)}, u32[]{:S(2)}, u32[]{:S(2)}) collective-permute-start(bf16[192,3072]{1,0:T(8,128)(2,1)S(1)} %bitcast.180), channel_id=1, source_target_pairs={{0,0},{1,4},{2,2},{3,6},{4,1},{5,5},{6,3},{7,7},{8,8},{9,12},{10,1... | collective-permute-start | bytes 3538952 | tf_op jit(solution)/shard_map/ppermute | solution.py:37
  11.6 95.4 %collective-permute-start.5 = (bf16[192,3072]{1,0:T(8,128)(2,1)S(1)}, bf16[192,3072]{1,0:T(8,128)(2,1)}, u32[]{:S(2)}, u32[]{:S(2)}) collective-permute-start(bf16[192,3072]{1,0:T(8,128)(2,1)S(1)} %bitcast.179), channel_id=1, source_target_pairs={{0,16},{1,20},{2,18},{3,22},{4,17},{5,21},{6,19},{7,23},{8,24},{9,... | collective-permute-start | bytes 3538952 | tf_op jit(solution)/shard_map/ppermute | solution.py:37
  58.4 49.2 %collective-permute-start.2 = (bf16[192,3072]{1,0:T(8,128)(2,1)}, bf16[192,3072]{1,0:T(8,128)(2,1)}, u32[]{:S(2)}, u32[]{:S(2)}) collective-permute-start(bf16[192,3072]{1,0:T(8,128)(2,1)} %collective-permute-done.1.refs_0_), channel_id=1, source_target_pairs={{0,2},{1,3},{2,0},{3,1},{4,6},{5,7},{6,4},{7,5},{8,10},{9,11},{10,... | collective-permute-start | bytes 3538952 | tf_op jit(solution)/shard_map/ppermute | solution.py:37
  59.7 105.2 %copy-start.6 = (bf16[192,3072]{1,0:T(8,128)(2,1)}, bf16[192,3072]{1,0:T(8,128)(2,1)S(1)}, u32[]{:S(2)}) copy-start(bf16[192,3072]{1,0:T(8,128)(2,1)S(1)} %collective-permute-done.9.refs_0_) | copy-start | bytes 3538948
  59.7 52.2 %collective-permute-start.10 = (bf16[192,3072]{1,0:T(8,128)(2,1)S(1)}, bf16[192,3072]{1,0:T(8,128)(2,1)S(1)}, u32[]{:S(2)}, u32[]{:S(2)}) collective-permute-start(bf16[192,3072]{1,0:T(8,128)(2,1)S(1)} %collective-permute-done.9.refs_0_), channel_id=1, source_target_pairs={{0,2},{1,3},{2,0},{3,1},{4,6},{5,7},{6,4},{7,5},{8,10},{9,11},{10,... | collective-permute-start | bytes 3538952 | tf_op jit(solution)/shard_map/ppermute | solution.py:37
  60.0 77.2 %collective-permute-start.14 = (bf16[192,3072]{1,0:T(8,128)(2,1)}, bf16[192,3072]{1,0:T(8,128)(2,1)}, u32[]{:S(2)}, u32[]{:S(2)}) collective-permute-start(bf16[192,3072]{1,0:T(8,128)(2,1)} %collective-permute-done.13.refs_0_), channel_id=1, source_target_pairs={{0,2},{1,3},{2,0},{3,1},{4,6},{5,7},{6,4},{7,5},{8,10},{9,11},{10,... | collective-permute-start | bytes 3538952 | tf_op jit(solution)/shard_map/ppermute | solution.py:37
  107.0 54.8 %collective-permute-start.6 = (bf16[192,3072]{1,0:T(8,128)(2,1)}, bf16[192,3072]{1,0:T(8,128)(2,1)}, u32[]{:S(2)}, u32[]{:S(2)}) collective-permute-start(bf16[192,3072]{1,0:T(8,128)(2,1)} %collective-permute-done.5.refs_0_), channel_id=1, source_target_pairs={{0,2},{1,3},{2,0},{3,1},{4,6},{5,7},{6,4},{7,5},{8,10},{9,11},{10,... | collective-permute-start | bytes 3538952 | tf_op jit(solution)/shard_map/ppermute | solution.py:37
  107.2 54.9 %collective-permute-start.11 = (bf16[192,3072]{1,0:T(8,128)(2,1)S(1)}, bf16[192,3072]{1,0:T(8,128)(2,1)S(1)}, u32[]{:S(2)}, u32[]{:S(2)}) collective-permute-start(bf16[192,3072]{1,0:T(8,128)(2,1)S(1)} %collective-permute-done.9.refs_0_), channel_id=1, source_target_pairs={{0,1},{1,0},{2,3},{3,2},{4,5},{5,4},{6,7},{7,6},{8,9},{9,8},{10,11... | collective-permute-start | bytes 3538952 | tf_op jit(solution)/shard_map/ppermute | solution.py:37
  107.6 56.8 %collective-permute-start.15 = (bf16[192,3072]{1,0:T(8,128)(2,1)}, bf16[192,3072]{1,0:T(8,128)(2,1)}, u32[]{:S(2)}, u32[]{:S(2)}) collective-permute-start(bf16[192,3072]{1,0:T(8,128)(2,1)} %collective-permute-done.13.refs_0_), channel_id=1, source_target_pairs={{0,1},{1,0},{2,3},{3,2},{4,5},{5,4},{6,7},{7,6},{8,9},{9,8},{10,11... | collective-permute-start | bytes 3538952 | tf_op jit(solution)/shard_map/ppermute | solution.py:37
  111.9 52.7 %collective-permute-start.12 = (bf16[192,3072]{1,0:T(8,128)(2,1)S(1)}, bf16[192,3072]{1,0:T(8,128)(2,1)}, u32[]{:S(2)}, u32[]{:S(2)}) collective-permute-start(bf16[192,3072]{1,0:T(8,128)(2,1)S(1)} %collective-permute-done.10.refs_1_), channel_id=1, source_target_pairs={{0,1},{1,0},{2,3},{3,2},{4,5},{5,4},{6,7},{7,6},{8,9},{9,8},{10,11... | collective-permute-start | bytes 3538952 | tf_op jit(solution)/shard_map/ppermute | solution.py:37
  137.1 27.7 %collective-permute-start.16 = (bf16[192,3072]{1,0:T(8,128)(2,1)}, bf16[192,3072]{1,0:T(8,128)(2,1)}, u32[]{:S(2)}, u32[]{:S(2)}) collective-permute-start(bf16[192,3072]{1,0:T(8,128)(2,1)} %collective-permute-done.14.refs_1_), channel_id=1, source_target_pairs={{0,1},{1,0},{2,3},{3,2},{4,5},{5,4},{6,7},{7,6},{8,9},{9,8},{10,11... | collective-permute-start | bytes 3538952 | tf_op jit(solution)/shard_map/ppermute | solution.py:37
  161.8 34.7 %collective-permute-start.7 = (bf16[192,3072]{1,0:T(8,128)(2,1)}, bf16[192,3072]{1,0:T(8,128)(2,1)S(1)}, u32[]{:S(2)}, u32[]{:S(2)}) collective-permute-start(bf16[192,3072]{1,0:T(8,128)(2,1)} %collective-permute-done.5.refs_0_), channel_id=1, source_target_pairs={{0,1},{1,0},{2,3},{3,2},{4,5},{5,4},{6,7},{7,6},{8,9},{9,8},{10,11... | collective-permute-start | bytes 3538952 | tf_op jit(solution)/shard_map/ppermute | solution.py:37
  162.1 34.3 %collective-permute-start.8 = (bf16[192,3072]{1,0:T(8,128)(2,1)}, bf16[192,3072]{1,0:T(8,128)(2,1)S(1)}, u32[]{:S(2)}, u32[]{:S(2)}) collective-permute-start(bf16[192,3072]{1,0:T(8,128)(2,1)} %collective-permute-done.6.refs_1_), channel_id=1, source_target_pairs={{0,1},{1,0},{2,3},{3,2},{4,5},{5,4},{6,7},{7,6},{8,9},{9,8},{10,11... | collective-permute-start | bytes 3538952 | tf_op jit(solution)/shard_map/ppermute | solution.py:37
  164.4 45.8 %collective-permute-start.3 = (bf16[192,3072]{1,0:T(8,128)(2,1)}, bf16[192,3072]{1,0:T(8,128)(2,1)S(1)}, u32[]{:S(2)}, u32[]{:S(2)}) collective-permute-start(bf16[192,3072]{1,0:T(8,128)(2,1)} %collective-permute-done.1.refs_0_), channel_id=1, source_target_pairs={{0,1},{1,0},{2,3},{3,2},{4,5},{5,4},{6,7},{7,6},{8,9},{9,8},{10,11... | collective-permute-start | bytes 3538952 | tf_op jit(solution)/shard_map/ppermute | solution.py:37
  164.6 68.4 %collective-permute-start.44 = (bf16[768,1536]{1,0:T(8,128)(2,1)S(1)}, bf16[768,1536]{1,0:T(8,128)(2,1)}, u32[]{:S(2)}, u32[]{:S(2)}) collective-permute-start(bf16[768,1536]{1,0:T(8,128)(2,1)S(1)} %constant_dynamic-slice_fusion), channel_id=1, source_target_pairs={{0,2},{1,3},{2,0},{3,1},{4,6},{5,7},{6,4},{7,5},{8,10},{9,11},{10,... | collective-permute-start | bytes 7077896 | tf_op jit(solution)/shard_map/ppermute | solution.py:37
  164.9 45.3 %collective-permute-start.4 = (bf16[192,3072]{1,0:T(8,128)(2,1)}, bf16[192,3072]{1,0:T(8,128)(2,1)S(1)}, u32[]{:S(2)}, u32[]{:S(2)}) collective-permute-start(bf16[192,3072]{1,0:T(8,128)(2,1)} %collective-permute-done.2.refs_1_), channel_id=1, source_target_pairs={{0,1},{1,0},{2,3},{3,2},{4,5},{5,4},{6,7},{7,6},{8,9},{9,8},{10,11... | collective-permute-start | bytes 3538952 | tf_op jit(solution)/shard_map/ppermute | solution.py:37
  226.8 21.1 %collective-permute-start.17 = (bf16[2,1536,128]{2,1,0:T(8,128)(2,1)S(1)}, bf16[2,1536,128]{2,1,0:T(8,128)(2,1)}, u32[]{:S(2)}, u32[]{:S(2)}) collective-permute-start(bf16[2,1536,128]{2,1,0:T(8,128)(2,1)S(1)} %get-tuple-element.70), channel_id=1, source_target_pairs={{0,8},{1,9},{2,10},{3,11},{4,12},{5,13},{6,14},{7,15},{8,16},{9,17... | collective-permute-start | bytes 2359304 | tf_op jit(solution)/shard_map/ppermute | solution.py:37
  229.8 21.1 %collective-permute-start.18 = (bf16[2,1536,128]{2,1,0:T(8,128)(2,1)S(1)}, bf16[2,1536,128]{2,1,0:T(8,128)(2,1)}, u32[]{:S(2)}, u32[]{:S(2)}) collective-permute-start(bf16[2,1536,128]{2,1,0:T(8,128)(2,1)S(1)} %get-tuple-element.71), channel_id=1, source_target_pairs={{8,0},{9,1},{10,2},{11,3},{12,4},{13,5},{14,6},{15,7},{16,8},{17,9... | collective-permute-start | bytes 2359304 | tf_op jit(solution)/shard_map/ppermute | solution.py:37
  233.0 111.3 %collective-permute-start.45 = (bf16[768,1536]{1,0:T(8,128)(2,1)}, bf16[768,1536]{1,0:T(8,128)(2,1)}, u32[]{:S(2)}, u32[]{:S(2)}) collective-permute-start(bf16[768,1536]{1,0:T(8,128)(2,1)} %collective-permute-done.44), channel_id=1, source_target_pairs={{0,1},{1,0},{2,3},{3,2},{4,5},{5,4},{6,7},{7,6},{8,9},{9,8},{10,11... | collective-permute-start | bytes 7077896 | tf_op jit(solution)/shard_map/ppermute | solution.py:37
  233.7 5.3 %collective-permute-start = (s32[32,7]{0,1:T(8,128)S(1)}, s32[32,7]{0,1:T(8,128)S(1)}, u32[]{:S(2)}, u32[]{:S(2)}) collective-permute-start(s32[32,7]{0,1:T(8,128)S(1)} %pad_add_fusion), channel_id=1, source_target_pairs={{0,0},{1,4},{2,2},{3,6},{4,1},{5,5},{6,3},{7,7},{8,8},{9,12},{10,1... | collective-permute-start | bytes 2696 | tf_op jit(solution)/shard_map/ppermute | solution.py:37
  235.6 38.8 %collective-permute-start.29 = (bf16[2,1536,128]{2,1,0:T(8,128)(2,1)}, bf16[2,1536,128]{2,1,0:T(8,128)(2,1)}, u32[]{:S(2)}, u32[]{:S(2)}) collective-permute-start(bf16[2,1536,128]{2,1,0:T(8,128)(2,1)} %get-tuple-element.76), channel_id=1, source_target_pairs={{0,8},{1,9},{2,10},{3,11},{4,12},{5,13},{6,14},{7,15},{8,16},{9,17... | collective-permute-start | bytes 2359304 | tf_op jit(solution)/shard_map/ppermute | solution.py:37
  239.0 38.5 %collective-permute-start.30 = (bf16[2,1536,128]{2,1,0:T(8,128)(2,1)}, bf16[2,1536,128]{2,1,0:T(8,128)(2,1)}, u32[]{:S(2)}, u32[]{:S(2)}) collective-permute-start(bf16[2,1536,128]{2,1,0:T(8,128)(2,1)} %get-tuple-element.77), channel_id=1, source_target_pairs={{8,0},{9,1},{10,2},{11,3},{12,4},{13,5},{14,6},{15,7},{16,8},{17,9... | collective-permute-start | bytes 2359304 | tf_op jit(solution)/shard_map/ppermute | solution.py:37
  247.9 51.6 %collective-permute-start.23 = (bf16[2,1536,128]{2,1,0:T(8,128)(2,1)}, bf16[2,1536,128]{2,1,0:T(8,128)(2,1)}, u32[]{:S(2)}, u32[]{:S(2)}) collective-permute-start(bf16[2,1536,128]{2,1,0:T(8,128)(2,1)} %copy-done.2), channel_id=1, source_target_pairs={{0,8},{1,9},{2,10},{3,11},{4,12},{5,13},{6,14},{7,15},{8,16},{9,17... | collective-permute-start | bytes 2359304 | tf_op jit(solution)/shard_map/ppermute | solution.py:37
  250.9 48.9 %collective-permute-start.24 = (bf16[2,1536,128]{2,1,0:T(8,128)(2,1)}, bf16[2,1536,128]{2,1,0:T(8,128)(2,1)}, u32[]{:S(2)}, u32[]{:S(2)}) collective-permute-start(bf16[2,1536,128]{2,1,0:T(8,128)(2,1)} %copy-done), channel_id=1, source_target_pairs={{8,0},{9,1},{10,2},{11,3},{12,4},{13,5},{14,6},{15,7},{16,8},{17,9... | collective-permute-start | bytes 2359304 | tf_op jit(solution)/shard_map/ppermute | solution.py:37
  274.5 46.7 %collective-permute-start.21 = (bf16[2,4,96,128]{3,2,0,1:T(8,128)(2,1)S(1)}, bf16[2,4,96,128]{3,2,0,1:T(8,128)(2,1)S(1)}, u32[]{:S(2)}, u32[]{:S(2)}) collective-permute-start(bf16[2,4,96,128]{3,2,0,1:T(8,128)(2,1)S(1)} %bitcast.206), channel_id=1, source_target_pairs={{0,3},{1,2},{2,1},{3,0},{4,7},{5,6},{6,5},{7,4},{8,11},{9,10},{10,... | collective-permute-start | bytes 589832 | tf_op jit(solution)/shard_map/ppermute | solution.py:37
  277.6 44.2 %collective-permute-start.20 = (bf16[2,4,96,128]{3,2,0,1:T(8,128)(2,1)S(1)}, bf16[2,4,96,128]{3,2,0,1:T(8,128)(2,1)S(1)}, u32[]{:S(2)}, u32[]{:S(2)}) collective-permute-start(bf16[2,4,96,128]{3,2,0,1:T(8,128)(2,1)S(1)} %bitcast.199), channel_id=1, source_target_pairs={{0,2},{1,3},{2,0},{3,1},{4,6},{5,7},{6,4},{7,5},{8,10},{9,11},{10,... | collective-permute-start | bytes 589832 | tf_op jit(solution)/shard_map/ppermute | solution.py:37
  299.5 22.8 %collective-permute-start.19 = (bf16[2,4,96,128]{3,2,0,1:T(8,128)(2,1)S(1)}, bf16[2,4,96,128]{3,2,0,1:T(8,128)(2,1)S(1)}, u32[]{:S(2)}, u32[]{:S(2)}) collective-permute-start(bf16[2,4,96,128]{3,2,0,1:T(8,128)(2,1)S(1)} %bitcast.201), channel_id=1, source_target_pairs={{0,1},{1,0},{2,3},{3,2},{4,5},{5,4},{6,7},{7,6},{8,9},{9,8},{10,11... | collective-permute-start | bytes 589832 | tf_op jit(solution)/shard_map/ppermute | solution.py:37
  299.8 23.7 %collective-permute-start.33 = (bf16[2,4,96,128]{3,2,0,1:T(8,128)(2,1)S(1)}, bf16[2,4,96,128]{3,2,0,1:T(8,128)(2,1)S(1)}, u32[]{:S(2)}, u32[]{:S(2)}) collective-permute-start(bf16[2,4,96,128]{3,2,0,1:T(8,128)(2,1)S(1)} %bitcast.200), channel_id=1, source_target_pairs={{0,3},{1,2},{2,1},{3,0},{4,7},{5,6},{6,5},{7,4},{8,11},{9,10},{10,... | collective-permute-start | bytes 589832 | tf_op jit(solution)/shard_map/ppermute | solution.py:37
  321.2 6.5 %collective-permute-start.32 = (bf16[2,4,96,128]{3,2,0,1:T(8,128)(2,1)S(1)}, bf16[2,4,96,128]{3,2,0,1:T(8,128)(2,1)S(1)}, u32[]{:S(2)}, u32[]{:S(2)}) collective-permute-start(bf16[2,4,96,128]{3,2,0,1:T(8,128)(2,1)S(1)} %bitcast.205), channel_id=1, source_target_pairs={{0,2},{1,3},{2,0},{3,1},{4,6},{5,7},{6,4},{7,5},{8,10},{9,11},{10,... | collective-permute-start | bytes 589832 | tf_op jit(solution)/shard_map/ppermute | solution.py:37
  321.7 7.4 %collective-permute-start.31 = (bf16[2,4,96,128]{3,2,0,1:T(8,128)(2,1)S(1)}, bf16[2,4,96,128]{3,2,0,1:T(8,128)(2,1)S(1)}, u32[]{:S(2)}, u32[]{:S(2)}) collective-permute-start(bf16[2,4,96,128]{3,2,0,1:T(8,128)(2,1)S(1)} %bitcast.207), channel_id=1, source_target_pairs={{0,1},{1,0},{2,3},{3,2},{4,5},{5,4},{6,7},{7,6},{8,9},{9,8},{10,11... | collective-permute-start | bytes 589832 | tf_op jit(solution)/shard_map/ppermute | solution.py:37
  322.3 10.2 %collective-permute-start.27 = (bf16[2,4,96,128]{3,2,0,1:T(8,128)(2,1)S(1)}, bf16[2,4,96,128]{3,2,0,1:T(8,128)(2,1)S(1)}, u32[]{:S(2)}, u32[]{:S(2)}) collective-permute-start(bf16[2,4,96,128]{3,2,0,1:T(8,128)(2,1)S(1)} %bitcast.204), channel_id=1, source_target_pairs={{0,3},{1,2},{2,1},{3,0},{4,7},{5,6},{6,5},{7,4},{8,11},{9,10},{10,... | collective-permute-start | bytes 589832 | tf_op jit(solution)/shard_map/ppermute | solution.py:37
  323.5 12.6 %collective-permute-start.26 = (bf16[2,4,96,128]{3,2,0,1:T(8,128)(2,1)S(1)}, bf16[2,4,96,128]{3,2,0,1:T(8,128)(2,1)S(1)}, u32[]{:S(2)}, u32[]{:S(2)}) collective-permute-start(bf16[2,4,96,128]{3,2,0,1:T(8,128)(2,1)S(1)} %bitcast.203), channel_id=1, source_target_pairs={{0,2},{1,3},{2,0},{3,1},{4,6},{5,7},{6,4},{7,5},{8,10},{9,11},{10,... | collective-permute-start | bytes 589832 | tf_op jit(solution)/shard_map/ppermute | solution.py:37
  327.7 8.4 %collective-permute-start.25 = (bf16[2,4,96,128]{3,2,0,1:T(8,128)(2,1)S(1)}, bf16[2,4,96,128]{3,2,0,1:T(8,128)(2,1)S(1)}, u32[]{:S(2)}, u32[]{:S(2)}) collective-permute-start(bf16[2,4,96,128]{3,2,0,1:T(8,128)(2,1)S(1)} %bitcast.202), channel_id=1, source_target_pairs={{0,1},{1,0},{2,3},{3,2},{4,5},{5,4},{6,7},{7,6},{8,9},{9,8},{10,11... | collective-permute-start | bytes 589832 | tf_op jit(solution)/shard_map/ppermute | solution.py:37
  329.1 23.9 %collective-permute-start.22 = (bf16[4,192,128]{2,1,0:T(8,128)(2,1)S(1)}, bf16[4,192,128]{2,1,0:T(8,128)(2,1)S(1)}, u32[]{:S(2)}, u32[]{:S(2)}) collective-permute-start(bf16[4,192,128]{2,1,0:T(8,128)(2,1)S(1)} %bitcast.190), channel_id=1, source_target_pairs={{0,0},{1,4},{2,2},{3,6},{4,1},{5,5},{6,3},{7,7},{8,8},{9,12},{10,1... | collective-permute-start | bytes 589832 | tf_op jit(solution)/shard_map/ppermute | solution.py:37
  336.4 18.9 %collective-permute-start.28 = (bf16[4,192,128]{2,1,0:T(8,128)(2,1)S(1)}, bf16[4,192,128]{2,1,0:T(8,128)(2,1)S(1)}, u32[]{:S(2)}, u32[]{:S(2)}) collective-permute-start(bf16[4,192,128]{2,1,0:T(8,128)(2,1)S(1)} %bitcast.215), channel_id=1, source_target_pairs={{0,0},{1,4},{2,2},{3,6},{4,1},{5,5},{6,3},{7,7},{8,8},{9,12},{10,1... | collective-permute-start | bytes 589832 | tf_op jit(solution)/shard_map/ppermute | solution.py:37
  338.4 24.6 %collective-permute-start.34 = (bf16[4,192,128]{2,1,0:T(8,128)(2,1)S(1)}, bf16[4,192,128]{2,1,0:T(8,128)(2,1)S(1)}, u32[]{:S(2)}, u32[]{:S(2)}) collective-permute-start(bf16[4,192,128]{2,1,0:T(8,128)(2,1)S(1)} %bitcast.214), channel_id=1, source_target_pairs={{0,0},{1,4},{2,2},{3,6},{4,1},{5,5},{6,3},{7,7},{8,8},{9,12},{10,1... | collective-permute-start | bytes 589832 | tf_op jit(solution)/shard_map/ppermute | solution.py:37
  342.0 21.0 %collective-permute-start.35 = (bf16[4,192,128]{2,1,0:T(8,128)(2,1)S(1)}, bf16[4,192,128]{2,1,0:T(8,128)(2,1)S(1)}, u32[]{:S(2)}, u32[]{:S(2)}) collective-permute-start(bf16[4,192,128]{2,1,0:T(8,128)(2,1)S(1)} %bitcast.188), channel_id=1, source_target_pairs={{0,8},{1,12},{2,10},{3,14},{4,9},{5,13},{6,11},{7,15},{8,0},{9,4},... | collective-permute-start | bytes 589832 | tf_op jit(solution)/shard_map/ppermute | solution.py:37
  344.4 22.2 %collective-permute-start.36 = (bf16[4,192,128]{2,1,0:T(8,128)(2,1)S(1)}, bf16[4,192,128]{2,1,0:T(8,128)(2,1)S(1)}, u32[]{:S(2)}, u32[]{:S(2)}) collective-permute-start(bf16[4,192,128]{2,1,0:T(8,128)(2,1)S(1)} %bitcast.213), channel_id=1, source_target_pairs={{0,8},{1,12},{2,10},{3,14},{4,9},{5,13},{6,11},{7,15},{8,0},{9,4},... | collective-permute-start | bytes 589832 | tf_op jit(solution)/shard_map/ppermute | solution.py:37
  352.3 55.5 %copy-start.12 = (f32[3072]{0:T(1024)S(1)}, f32[3072]{0:T(1024)}, u32[]{:S(2)}) copy-start(f32[3072]{0:T(1024)} %param.7) | copy-start | bytes 36868
  353.0 13.6 %collective-permute-start.37 = (bf16[4,192,128]{2,1,0:T(8,128)(2,1)S(1)}, bf16[4,192,128]{2,1,0:T(8,128)(2,1)S(1)}, u32[]{:S(2)}, u32[]{:S(2)}) collective-permute-start(bf16[4,192,128]{2,1,0:T(8,128)(2,1)S(1)} %bitcast.212), channel_id=1, source_target_pairs={{0,8},{1,12},{2,10},{3,14},{4,9},{5,13},{6,11},{7,15},{8,0},{9,4},... | collective-permute-start | bytes 589832 | tf_op jit(solution)/shard_map/ppermute | solution.py:37
  355.4 28.5 %collective-permute-start.38 = (bf16[4,192,128]{2,1,0:T(8,128)(2,1)S(1)}, bf16[4,192,128]{2,1,0:T(8,128)(2,1)S(1)}, u32[]{:S(2)}, u32[]{:S(2)}) collective-permute-start(bf16[4,192,128]{2,1,0:T(8,128)(2,1)S(1)} %bitcast.187), channel_id=1, source_target_pairs={{0,16},{1,20},{2,18},{3,22},{4,17},{5,21},{6,19},{7,23},{8,24},{9,... | collective-permute-start | bytes 589832 | tf_op jit(solution)/shard_map/ppermute | solution.py:37
  363.0 25.1 %collective-permute-start.39 = (bf16[4,192,128]{2,1,0:T(8,128)(2,1)S(1)}, bf16[4,192,128]{2,1,0:T(8,128)(2,1)S(1)}, u32[]{:S(2)}, u32[]{:S(2)}) collective-permute-start(bf16[4,192,128]{2,1,0:T(8,128)(2,1)S(1)} %bitcast.211), channel_id=1, source_target_pairs={{0,16},{1,20},{2,18},{3,22},{4,17},{5,21},{6,19},{7,23},{8,24},{9,... | collective-permute-start | bytes 589832 | tf_op jit(solution)/shard_map/ppermute | solution.py:37
  363.1 31.3 %collective-permute-start.40 = (bf16[4,192,128]{2,1,0:T(8,128)(2,1)S(1)}, bf16[4,192,128]{2,1,0:T(8,128)(2,1)S(1)}, u32[]{:S(2)}, u32[]{:S(2)}) collective-permute-start(bf16[4,192,128]{2,1,0:T(8,128)(2,1)S(1)} %bitcast.210), channel_id=1, source_target_pairs={{0,16},{1,20},{2,18},{3,22},{4,17},{5,21},{6,19},{7,23},{8,24},{9,... | collective-permute-start | bytes 589832 | tf_op jit(solution)/shard_map/ppermute | solution.py:37
  366.6 35.8 %collective-permute-start.41 = (bf16[4,192,128]{2,1,0:T(8,128)(2,1)S(1)}, bf16[4,192,128]{2,1,0:T(8,128)(2,1)S(1)}, u32[]{:S(2)}, u32[]{:S(2)}) collective-permute-start(bf16[4,192,128]{2,1,0:T(8,128)(2,1)S(1)} %bitcast.186), channel_id=1, source_target_pairs={{0,24},{1,28},{2,26},{3,30},{4,25},{5,29},{6,27},{7,31},{8,16},{9,... | collective-permute-start | bytes 589832 | tf_op jit(solution)/shard_map/ppermute | solution.py:37
  366.6 39.1 %collective-permute-start.42 = (bf16[4,192,128]{2,1,0:T(8,128)(2,1)S(1)}, bf16[4,192,128]{2,1,0:T(8,128)(2,1)S(1)}, u32[]{:S(2)}, u32[]{:S(2)}) collective-permute-start(bf16[4,192,128]{2,1,0:T(8,128)(2,1)S(1)} %bitcast.209), channel_id=1, source_target_pairs={{0,24},{1,28},{2,26},{3,30},{4,25},{5,29},{6,27},{7,31},{8,16},{9,... | collective-permute-start | bytes 589832 | tf_op jit(solution)/shard_map/ppermute | solution.py:37
  383.9 24.0 %collective-permute-start.43 = (bf16[4,192,128]{2,1,0:T(8,128)(2,1)S(1)}, bf16[4,192,128]{2,1,0:T(8,128)(2,1)S(1)}, u32[]{:S(2)}, u32[]{:S(2)}) collective-permute-start(bf16[4,192,128]{2,1,0:T(8,128)(2,1)S(1)} %bitcast.208), channel_id=1, source_target_pairs={{0,24},{1,28},{2,26},{3,30},{4,25},{5,29},{6,27},{7,31},{8,16},{9,... | collective-permute-start | bytes 589832 | tf_op jit(solution)/shard_map/ppermute | solution.py:37
  (15 other events, 286.5 us)
